TPU v7x, 32 devices: a whole 2x2x4 slice. The times are simulated.
32 devices in a mesh: lat: 4 (over x, core), lon: 8 (over z, y).
Axes of the slice: x: 2, y: 2, z: 4, core: 2. Of those that a mesh axis runs over, the one named last changes fastest.
Arguments:
- inputs_below: bfloat16 [64, 32, 1024], P(None, 'lat', 'lon'), may hold values from -6 to 6
- hidden_prev: bfloat16 [64, 32, 1024], P(None, 'lat', 'lon'), may hold values from -0.8984375 to 0.8984375
- cell_prev: float32 [64, 32, 1024], P(None, 'lat', 'lon'), may hold values from -5 to 5
- kernel_weights: bfloat16 [9, 256, 128], replicated, may hold values from -0.1875 to 0.1875
- gate_bias: float32 [256], replicated, may hold values from -4 to 4
- readout: float32 [64], replicated, may hold values from -0.75 to 0.75
- target_field: float32 [32, 1024], P('lat', 'lon'), may hold values from -6 to 6
- land_mask: int32 [32, 1024], P('lat', 'lon'), may hold values 0 or 1
- fire_mask: int32 [32, 1024], P('lat', 'lon'), may hold values 0 or 1
- hidden_grad: bfloat16 [64, 32, 1024], P(None, 'lat', 'lon'), may hold values from -10 to 10
Outputs:
- hidden_next: bfloat16 [64, 32, 1024], P(None, 'lat', 'lon')
- cell_next: float32 [64, 32, 1024], P(None, 'lat', 'lon')
- grad_inputs: bfloat16 [64, 32, 1024], P(None, 'lat', 'lon')
- grad_hidden: bfloat16 [64, 32, 1024], P(None, 'lat', 'lon')
- grad_cell: float32 [64, 32, 1024], P(None, 'lat', 'lon')
- grad_kernel: float32 [9, 256, 128], replicated
- grad_bias: float32 [256], replicated
Inputs may be any that keep to these rules, and one draw needn't show every extreme that they name: `land_mask`: 1 marks land cells, 0 sea cells. `fire_mask`: 1 marks cells where fire danger is observed.
All inputs are finite; a program needn't handle non-finite values. No bound on the sum of `land_mask` or of `fire_mask` on one device may be relied on, other than what follows from the above.
Results may differ from a plain program's by a relative error of at most 0.0049.
Values may be sent and summed in bfloat16 or wider, within the bound.
No kernel may reach another device: no remote copies, remote signals or barrier semaphores. Data moves between devices by JAX's collectives and lax.ppermute only.
A program may use at most 64 MiB of HBM per device.

v0:
```python
import math

import jax
import jax.numpy as jnp
from jax import lax
from jax.sharding import PartitionSpec as P


def with_halo(cells, sides, width, closed):
    for axis, dim in sides:
        count = lax.axis_size(axis)
        ends = count if closed else count - 1
        head = lax.slice_in_dim(cells, 0, width, axis=dim)
        tail = lax.slice_in_dim(cells, cells.shape[dim] - width, cells.shape[dim], axis=dim)
        cells = jnp.concatenate(
            [
                lax.ppermute(tail, axis, [(i, (i + 1) % count) for i in range(ends)]),
                cells,
                lax.ppermute(head, axis, [((i + 1) % count, i) for i in range(ends)]),
            ],
            axis=dim,
        )
    return cells


def shifted(value, axis, steps):
    count = lax.axis_size(axis)
    pairs = [(source, (source + steps) % count) for source in range(count)]
    return lax.ppermute(value, axis, pairs)


def extend(field):
    banded = with_halo(field, (("lat", 1),), 1, False)
    edge_rows = jnp.concatenate([field[:, :1], field[:, -1:]], axis=1)
    across = shifted(edge_rows, "lon", lax.axis_size("lon") // 2)
    band_index = lax.axis_index("lat")
    northern = band_index == 0
    southern = band_index == lax.axis_size("lat") - 1
    top_row = jnp.where(northern, across[:, :1], banded[:, :1])
    bottom_row = jnp.where(southern, across[:, 1:], banded[:, -1:])
    joined = jnp.concatenate([top_row, banded[:, 1:-1], bottom_row], axis=1)
    return with_halo(joined, (("lon", 2),), 1, True)


def windows(padded, row_count, col_count, flipped):
    result = []
    for position in range(9):
        lat_start = position // 3
        lon_start = position % 3
        if flipped:
            lat_start = 2 - lat_start
            lon_start = 2 - lon_start
        result.append(
            padded[:, lat_start : lat_start + row_count, lon_start : lon_start + col_count]
        )
    return result


def body(
    inputs_below,
    hidden_prev,
    cell_prev,
    kernel_weights,
    gate_bias,
    readout,
    target_field,
    land_mask,
    fire_mask,
    hidden_grad,
):
    hidden_width = hidden_prev.shape[0]
    input_width = inputs_below.shape[0]
    gate_count = kernel_weights.shape[1]
    channels = kernel_weights.shape[2]
    row_count = cell_prev.shape[1]
    col_count = cell_prev.shape[2]
    stacked = jnp.concatenate([inputs_below, hidden_prev], axis=0)
    padded = extend(stacked)
    forward_windows = windows(padded, row_count, col_count, False)
    patches = jnp.concatenate(forward_windows, axis=0)
    flat_kernel = jnp.transpose(kernel_weights, (1, 0, 2)).reshape(gate_count, 9 * channels)
    preact = jnp.einsum("gk,krw->grw", flat_kernel, patches, preferred_element_type=jnp.float32)
    preact = preact + gate_bias[:, None, None]
    input_gate = jax.nn.sigmoid(preact[0:hidden_width])
    forget_gate = jax.nn.sigmoid(preact[hidden_width : 2 * hidden_width])
    output_gate = jax.nn.sigmoid(preact[2 * hidden_width : 3 * hidden_width])
    candidate = jnp.tanh(preact[3 * hidden_width : 4 * hidden_width])
    land_float = land_mask.astype(jnp.float32)[None]
    fire_float = fire_mask.astype(jnp.float32)
    cell_next = land_float * (forget_gate * cell_prev + input_gate * candidate)
    squashed = jnp.tanh(cell_next)
    hidden_next = (output_gate * squashed).astype(jnp.bfloat16)
    predicted = jnp.sum(readout[:, None, None] * hidden_next.astype(jnp.float32), axis=0)
    total_grad = (
        hidden_grad.astype(jnp.float32)
        + 2.0 * (fire_float * (predicted - target_field))[None] * readout[:, None, None]
    )
    cell_grad = land_float * total_grad * output_gate * (1.0 - squashed * squashed)
    grad_cell = cell_grad * forget_gate
    pre_grad = jnp.concatenate(
        [
            cell_grad * candidate * input_gate * (1.0 - input_gate),
            cell_grad * cell_prev * forget_gate * (1.0 - forget_gate),
            total_grad * squashed * output_gate * (1.0 - output_gate),
            cell_grad * input_gate * (1.0 - candidate * candidate),
        ],
        axis=0,
    )
    pre_low = pre_grad.astype(jnp.bfloat16)
    local_bias = jnp.sum(pre_grad, axis=(1, 2))
    local_kernel = jnp.transpose(
        jnp.einsum("grw,krw->gk", pre_low, patches, preferred_element_type=jnp.float32).reshape(
            gate_count, 9, channels
        ),
        (1, 0, 2),
    )
    grad_padded = extend(pre_low)
    band_index = lax.axis_index("lat")
    northern = band_index == 0
    southern = band_index == lax.axis_size("lat") - 1
    row_index = lax.broadcasted_iota(jnp.int32, (1, row_count + 2, 1), 1)
    pole_rows = northern & (row_index == 0) | southern & (row_index == row_count + 1)
    main_padded = jnp.where(pole_rows, jnp.zeros_like(grad_padded), grad_padded)
    back_windows = windows(main_padded, row_count, col_count, True)
    back_patches = jnp.concatenate(back_windows, axis=0)
    flat_back = jnp.transpose(kernel_weights, (2, 0, 1)).reshape(channels, 9 * gate_count)
    field_grad = jnp.einsum(
        "ck,krw->crw", flat_back, back_patches, preferred_element_type=jnp.float32
    )
    north_term = jnp.zeros((channels, col_count), jnp.float32)
    south_term = jnp.zeros((channels, col_count), jnp.float32)
    for position in range(3):
        lon_start = 2 - position
        north_term = north_term + jnp.einsum(
            "gc,gw->cw",
            kernel_weights[position],
            grad_padded[:, 0, lon_start : lon_start + col_count],
            preferred_element_type=jnp.float32,
        )
        south_term = south_term + jnp.einsum(
            "gc,gw->cw",
            kernel_weights[6 + position],
            grad_padded[:, row_count + 1, lon_start : lon_start + col_count],
            preferred_element_type=jnp.float32,
        )
    field_grad = field_grad.at[:, 0].add(jnp.where(northern, north_term, 0.0))
    field_grad = field_grad.at[:, row_count - 1].add(jnp.where(southern, south_term, 0.0))
    grad_inputs = field_grad[:input_width].astype(jnp.bfloat16)
    grad_hidden = field_grad[input_width:].astype(jnp.bfloat16)
    scaling = 1.0 / math.sqrt(row_count * lax.axis_size("lat") * col_count * lax.axis_size("lon"))
    summed_kernel, summed_bias = lax.psum((local_kernel, local_bias), ("lat", "lon"))
    grad_kernel = summed_kernel * scaling
    grad_bias = summed_bias * scaling
    return (hidden_next, cell_next, grad_inputs, grad_hidden, grad_cell, grad_kernel, grad_bias)


def solution(mesh):
    return jax.shard_map(
        body,
        mesh=mesh,
        in_specs=(
            P(None, "lat", "lon"),
            P(None, "lat", "lon"),
            P(None, "lat", "lon"),
            P(),
            P(),
            P(),
            P("lat", "lon"),
            P("lat", "lon"),
            P("lat", "lon"),
            P(None, "lat", "lon"),
        ),
        out_specs=(
            P(None, "lat", "lon"),
            P(None, "lat", "lon"),
            P(None, "lat", "lon"),
            P(None, "lat", "lon"),
            P(None, "lat", "lon"),
            P(),
            P(),
        ),
        check_vma=False,
    )
```

profile of v0, /device:TPU:0, one launch (start us, length us, event | category | flops | bytes accessed | tf_op | source)
XLA Modules:
  0.0 249.4 jit_solution(2983188765524370888)
XLA Ops:
  7.2 1.1 copy.112
  8.3 1.1 copy.113
  9.5 2.4 collective-permute-start.1
  11.9 1.3 collective-permute-start.2
  13.2 3.5 %collective-permute-start = (bf16[128,2,128]{0,2,1:T(8,128)(2,1)S(1)}, bf16[128,2,128]{0,2,1:T(8,128)(2,1)S(1)}, u32[]{:S(2)}, u32[]{:S(2)}) collective-permute-start(bf16[128,2,128]{0,2,1:T(8,128)(2,1)S(1)} %pad_maximum_fusion.16), channel_id=1, source_target_pairs={{0,4},{1,5},{2,6},{3,7},{4,0},{5,1},{6,2},{7,3},{8,12},{9,13},{10,... | collective-permute-start | bytes 196616 | tf_op jit(solution)/shard_map/ppermute | solution.py:29
  16.7 0.7 convert_element_type.20
  17.4 1.3 copy.116
  19.0 5.5 %collective-permute-start.4 = (bf16[128,10,1]{0,2,1:T(2,128)(2,1)S(1)}, bf16[128,10,1]{0,2,1:T(2,128)(2,1)S(1)}, u32[]{:S(2)}, u32[]{:S(2)}) collective-permute-start(bf16[128,10,1]{0,2,1:T(2,128)(2,1)S(1)} %get-tuple-element.92), channel_id=1, source_target_pairs={{1,0},{2,1},{3,2},{4,3},{5,4},{6,5},{7,6},{0,7},{9,8},{10,9},{11,1... | collective-permute-start | bytes 7688 | tf_op jit(solution)/shard_map/ppermute | solution.py:19
  24.6 1.0 pad_maximum_fusion.3
  25.6 0.3 collective-permute-done.4
  25.9 5.0 %collective-permute-done.3 = bf16[128,10,1]{0,2,1:T(2,128)(2,1)S(1)} collective-permute-done((bf16[128,10,1]{0,2,1:T(2,128)(2,1)S(1)}, bf16[128,10,1]{0,2,1:T(2,128)(2,1)S(1)}, u32[]{:S(2)}, u32[]{:S(2)}) %collective-permute-start.3) | collective-permute-done | bytes 2592 | tf_op jit(solution)/shard_map/ppermute | solution.py:17
  30.9 0.3 pad_maximum_fusion.2
  31.3 1.2 fusion.52
  32.5 3.9 %concatenate.64 = bf16[1152,8,128]{0,2,1:T(8,128)(2,1)S(1)} concatenate(bf16[128,8,128]{0,2,1:T(8,128)(2,1)} %get-tuple-element.112, bf16[128,8,128]{0,2,1:T(8,128)(2,1)} %get-tuple-element.97, bf16[128,8,128]{0,2,1:T(8,128)(2,1)} %get-tuple-element.102, bf16[128,8,128]{0,2,1:T(8,128)(2,1)} %get-tuple-element.113, bf16[64,8,128]{0,2,1:T(8,128)(2,1)S(1)} %copy.112, ...), dimensions={0} | concatenate | bytes 4718592 | tf_op jit(solution)/shard_map/concatenate | solution.py:80
  36.5 1.8 fusion.55
  38.3 1.6 copy.118
  39.9 0.3 add_bitcast_fusion
  40.3 1.9 multiply_reduce_fusion
  42.2 1.9 fusion.49
  44.5 0.8 fusion.51
  45.3 2.7 %collective-permute-start.6 = (bf16[256,1,128]{2,1,0:T(2,128)(2,1)}, bf16[256,1,128]{2,1,0:T(2,128)(2,1)}, u32[]{:S(2)}, u32[]{:S(2)}) collective-permute-start(bf16[256,1,128]{2,1,0:T(2,128)(2,1)} %get-tuple-element.94), channel_id=1, source_target_pairs={{0,8},{8,16},{16,24},{1,9},{9,17},{17,25},{2,10},{10,18},{18,26},{... | collective-permute-start | bytes 196616 | tf_op jit(solution)/shard_map/ppermute | solution.py:17
  48.0 1.8 pad_maximum_fusion.15
  49.8 1.3 collective-permute-start.7
  51.2 2.0 fusion.12
  53.2 1.0 fusion.10
  54.2 43.5 %psum.15 = f32[256]{0:T(256)S(1)} all-reduce(f32[256]{0:T(256)S(1)} %fusion.10), channel_id=1, replica_groups=mesh['lat'=4,'lon'=8] {'lat','lon'}, use_global_device_ids=true, to_apply=%region_3.4 | all-reduce | flops 256 | bytes 2048 | tf_op jit(solution)/shard_map/psum | solution.py:151
  97.7 1.3 broadcast_select_fusion.1
  99.0 0.6 pad_maximum_fusion.1
  99.7 0.5 fusion.50
  100.2 0.9 copy.119
  101.1 0.9 copy.120
  102.0 4.0 %collective-permute-start.9 = (bf16[256,10,1]{0,1,2:T(8,128)(2,1)S(1)}, bf16[256,10,1]{0,1,2:T(8,128)(2,1)S(1)}, u32[]{:S(2)}, u32[]{:S(2)}) collective-permute-start(bf16[256,10,1]{0,1,2:T(8,128)(2,1)S(1)} %copy.120), channel_id=1, source_target_pairs={{1,0},{2,1},{3,2},{4,3},{5,4},{6,5},{7,6},{0,7},{9,8},{10,9},{11,1... | collective-permute-start | bytes 15368 | tf_op jit(solution)/shard_map/ppermute | solution.py:19
  106.0 0.6 broadcast_multiply_fusion.1
  106.5 5.8 %collective-permute-done.8 = bf16[256,10,1]{0,1,2:T(8,128)(2,1)S(1)} collective-permute-done((bf16[256,10,1]{0,1,2:T(8,128)(2,1)S(1)}, bf16[256,10,1]{0,1,2:T(8,128)(2,1)S(1)}, u32[]{:S(2)}, u32[]{:S(2)}) %collective-permute-start.8) | collective-permute-done | bytes 5152 | tf_op jit(solution)/shard_map/ppermute | solution.py:17
  112.3 1.0 copy.121
  113.3 1.0 copy.122
  114.4 1.5 pad_maximum_fusion.7
  115.9 2.7 %maximum_select_fusion = bf16[256,10,130]{2,1,0:T(8,128)(2,1)S(1)} fusion(bf16[256,10,1]{2,1,0:T(8,128)(2,1)S(1)} %copy.122, bf16[256,1,128]{2,1,0:T(2,128)(2,1)S(1)} %get-tuple-element.109, bf16[256,8,128]{2,1,0:T(8,128)(2,1)S(1)} %fusion.11, bf16[256,1,128]{2,1,0:T(2,128)(2,1)S(1)} %get-tuple-element.108, bf16[256,10,1]{2,1,0:T(8,128)(2,1)S(1)} %copy.121, ...), kind=kLoop, calls=%fused_computation.2 | loop fusion | flops 3660800 | bytes 1331210 | tf_op jit(solution)/shard_map/jit(_where)/select_n | solution.py:123
  119.3 0.4 slice_dynamic-update-slice_fusion.8
  119.7 0.5 slice_dynamic-update-slice_fusion.7
  120.4 0.5 slice_dynamic-update-slice_fusion.5
  120.9 0.5 slice_dynamic-update-slice_fusion.4
  122.3 0.8 fusion
  124.0 0.7 copy.131
  124.7 0.7 copy.130
  125.5 114.3 %all-reduce.2.cloned.1.call-done = f32[9,256,128]{1,2,0:T(8,128)} async-done(((f32[9,256,128]{1,2,0:T(8,128)}), f32[9,256,128]{1,2,0:T(8,128)}) %all-reduce.2.cloned.1.call-update) | async-done | bytes 1179664 | tf_op jit(solution)/shard_map/psum | solution.py:151
  239.7 1.4 broadcast_multiply_fusion
  241.1 1.4 copy.132
  (48 shorter events, 3.4 us)
Async XLA Ops:
  7.2 232.6 %all-reduce.2.cloned.1.call-start = ((), (), s32[]{:S(2)}) async-start(), calls=%async_computation | async-start | bytes 2359296 | tf_op jit(solution)/shard_map/psum | solution.py:151
  9.5 9.2 %collective-permute-start.1 = (bf16[128,1,128]{0,2,1:T(8,128)(2,1)S(1)}, bf16[128,1,128]{0,2,1:T(8,128)(2,1)S(1)}, u32[]{:S(2)}, u32[]{:S(2)}) collective-permute-start(bf16[128,1,128]{0,2,1:T(8,128)(2,1)S(1)} %get-tuple-element.98), channel_id=1, source_target_pairs={{0,8},{8,16},{16,24},{1,9},{9,17},{17,25},{2,10},{10,18},{18,26},{... | collective-permute-start | bytes 98312 | tf_op jit(solution)/shard_map/ppermute | solution.py:17
  11.9 6.8 %collective-permute-start.2 = (bf16[128,1,128]{0,2,1:T(8,128)(2,1)S(1)}, bf16[128,1,128]{0,2,1:T(8,128)(2,1)S(1)}, u32[]{:S(2)}, u32[]{:S(2)}) collective-permute-start(bf16[128,1,128]{0,2,1:T(8,128)(2,1)S(1)} %get-tuple-element.99), channel_id=1, source_target_pairs={{8,0},{16,8},{24,16},{9,1},{17,9},{25,17},{10,2},{18,10},{26,18},{... | collective-permute-start | bytes 98312 | tf_op jit(solution)/shard_map/ppermute | solution.py:19
  13.2 5.7 %collective-permute-start = (bf16[128,2,128]{0,2,1:T(8,128)(2,1)S(1)}, bf16[128,2,128]{0,2,1:T(8,128)(2,1)S(1)}, u32[]{:S(2)}, u32[]{:S(2)}) collective-permute-start(bf16[128,2,128]{0,2,1:T(8,128)(2,1)S(1)} %pad_maximum_fusion.16), channel_id=1, source_target_pairs={{0,4},{1,5},{2,6},{3,7},{4,0},{5,1},{6,2},{7,3},{8,12},{9,13},{10,... | collective-permute-start | bytes 196616 | tf_op jit(solution)/shard_map/ppermute | solution.py:29
  19.0 6.9 %collective-permute-start.4 = (bf16[128,10,1]{0,2,1:T(2,128)(2,1)S(1)}, bf16[128,10,1]{0,2,1:T(2,128)(2,1)S(1)}, u32[]{:S(2)}, u32[]{:S(2)}) collective-permute-start(bf16[128,10,1]{0,2,1:T(2,128)(2,1)S(1)} %get-tuple-element.92), channel_id=1, source_target_pairs={{1,0},{2,1},{3,2},{4,3},{5,4},{6,5},{7,6},{0,7},{9,8},{10,9},{11,1... | collective-permute-start | bytes 7688 | tf_op jit(solution)/shard_map/ppermute | solution.py:19
  24.6 6.4 %collective-permute-start.3 = (bf16[128,10,1]{0,2,1:T(2,128)(2,1)S(1)}, bf16[128,10,1]{0,2,1:T(2,128)(2,1)S(1)}, u32[]{:S(2)}, u32[]{:S(2)}) collective-permute-start(bf16[128,10,1]{0,2,1:T(2,128)(2,1)S(1)} %get-tuple-element.93), channel_id=1, source_target_pairs={{0,1},{1,2},{2,3},{3,4},{4,5},{5,6},{6,7},{7,0},{8,9},{9,10},{10,1... | collective-permute-start | bytes 7688 | tf_op jit(solution)/shard_map/ppermute | solution.py:17
  36.4 3.5 %copy-start.6 = (f32[256]{0:T(256)S(1)}, f32[256]{0:T(256)}, u32[]{:S(2)}) copy-start(f32[256]{0:T(256)} %param.18) | copy-start | bytes 3076
  36.4 3.9 %copy-start.5 = (f32[64]{0:T(128)S(1)}, f32[64]{0:T(128)}, u32[]{:S(2)}) copy-start(f32[64]{0:T(128)} %param.19) | copy-start | bytes 772
  36.4 5.8 %copy-start.3 = (f32[8,128]{1,0:T(8,128)S(1)}, f32[8,128]{1,0:T(8,128)}, u32[]{:S(2)}) copy-start(f32[8,128]{1,0:T(8,128)} %param.20) | copy-start | bytes 12292
  36.4 5.8 %copy-start.4 = (s32[8,128]{1,0:T(8,128)S(1)}, s32[8,128]{1,0:T(8,128)}, u32[]{:S(2)}) copy-start(s32[8,128]{1,0:T(8,128)} %param.22) | copy-start | bytes 12292
  39.9 4.2 %copy-start.2 = (f32[64,8,128]{2,1,0:T(8,128)S(1)}, f32[64,8,128]{2,1,0:T(8,128)}, u32[]{:S(2)}) copy-start(f32[64,8,128]{2,1,0:T(8,128)} %param.16) | copy-start | bytes 786436
  42.2 2.2 copy-start.1
  45.3 52.4 %collective-permute-start.6 = (bf16[256,1,128]{2,1,0:T(2,128)(2,1)}, bf16[256,1,128]{2,1,0:T(2,128)(2,1)}, u32[]{:S(2)}, u32[]{:S(2)}) collective-permute-start(bf16[256,1,128]{2,1,0:T(2,128)(2,1)} %get-tuple-element.94), channel_id=1, source_target_pairs={{0,8},{8,16},{16,24},{1,9},{9,17},{17,25},{2,10},{10,18},{18,26},{... | collective-permute-start | bytes 196616 | tf_op jit(solution)/shard_map/ppermute | solution.py:17
  49.8 47.9 %collective-permute-start.7 = (bf16[256,1,128]{2,1,0:T(2,128)(2,1)S(1)}, bf16[256,1,128]{2,1,0:T(2,128)(2,1)}, u32[]{:S(2)}, u32[]{:S(2)}) collective-permute-start(bf16[256,1,128]{2,1,0:T(2,128)(2,1)S(1)} %get-tuple-element.95), channel_id=1, source_target_pairs={{8,0},{16,8},{24,16},{9,1},{17,9},{25,17},{10,2},{18,10},{26,18},{... | collective-permute-start | bytes 196616 | tf_op jit(solution)/shard_map/ppermute | solution.py:19
  51.1 46.6 %collective-permute-start.5 = (bf16[256,2,128]{2,1,0:T(2,128)(2,1)}, bf16[256,2,128]{2,1,0:T(2,128)(2,1)S(1)}, u32[]{:S(2)}, u32[]{:S(2)}) collective-permute-start(bf16[256,2,128]{2,1,0:T(2,128)(2,1)} %pad_maximum_fusion.15), channel_id=1, source_target_pairs={{0,4},{1,5},{2,6},{3,7},{4,0},{5,1},{6,2},{7,3},{8,12},{9,13},{10,... | collective-permute-start | bytes 393224 | tf_op jit(solution)/shard_map/ppermute | solution.py:29
  102.0 11.4 %collective-permute-start.9 = (bf16[256,10,1]{0,1,2:T(8,128)(2,1)S(1)}, bf16[256,10,1]{0,1,2:T(8,128)(2,1)S(1)}, u32[]{:S(2)}, u32[]{:S(2)}) collective-permute-start(bf16[256,10,1]{0,1,2:T(8,128)(2,1)S(1)} %copy.120), channel_id=1, source_target_pairs={{1,0},{2,1},{3,2},{4,3},{5,4},{6,5},{7,6},{0,7},{9,8},{10,9},{11,1... | collective-permute-start | bytes 15368 | tf_op jit(solution)/shard_map/ppermute | solution.py:19
  106.0 6.3 %collective-permute-start.8 = (bf16[256,10,1]{0,1,2:T(8,128)(2,1)S(1)}, bf16[256,10,1]{0,1,2:T(8,128)(2,1)S(1)}, u32[]{:S(2)}, u32[]{:S(2)}) collective-permute-start(bf16[256,10,1]{0,1,2:T(8,128)(2,1)S(1)} %copy.119), channel_id=1, source_target_pairs={{0,1},{1,2},{2,3},{3,4},{4,5},{5,6},{6,7},{7,0},{8,9},{9,10},{10,1... | collective-permute-start | bytes 15368 | tf_op jit(solution)/shard_map/ppermute | solution.py:17
  114.4 4.3 %copy-start = (bf16[9,256,128]{2,1,0:T(8,128)(2,1)S(1)}, bf16[9,256,128]{2,1,0:T(8,128)(2,1)}, u32[]{:S(2)}) copy-start(bf16[9,256,128]{2,1,0:T(8,128)(2,1)} %param.17) | copy-start | bytes 1769476
Sparse Core Ops, SparseCore 0:
  106.7 133.0 all-reduce.1
where the time goes:
time: 250 us; the launch traced here: 249 us
  waiting for transfers between devices  126 us (50%)
  blocking collectives  43.5 us (17%)
  local copies, waits for them, and re-layouts  21.4 us (9%)
  starting transfers between devices  20.7 us (8%)
  other arithmetic  17.8 us (7%)
  between operations  14.4 us (6%)
  matrix products  6.02 us (2%)
    psum x1, waiting for transfers between devices, body(): lax.psum((local_kernel, local_bias), ('lat', 'lon'))  114 us
    psum x1, blocking collectives, body(): lax.psum((local_kernel, local_bias), ('lat', 'lon'))  43.5 us
    ppermute x4, starting transfers between devices, with_halo(): lax.ppermute(head, axis, [((i + 1) % count, i) for i in range(ends)])  12.1 us
    ppermute x4, waiting for transfers between devices, with_halo(): lax.ppermute(tail, axis, [(i, (i + 1) % count) for i in range(ends)])  10.8 us
    unnamed x29, local copies, waits for them, and re-layouts  9.34 us
    ppermute x4, starting transfers between devices, with_halo(): lax.ppermute(tail, axis, [(i, (i + 1) % count) for i in range(ends)])  5.03 us
  transfers between devices with their start and end apart: 11, of which 5 were waited for; matrix products, arithmetic and copies ran while one was open for 9% of the time, Pallas kernels for 0%

commit v1 on v0

v1 whole, which is shorter than its diff:
```python
import functools
import math

import jax
import jax.numpy as jnp
from jax import lax
from jax.experimental import pallas as pl
from jax.experimental.pallas import tpu as pltpu
from jax.sharding import PartitionSpec as P

F32 = jnp.float32
BF16 = jnp.bfloat16
AXES = ("lat", "lon")
BIAS_ROWS = 16
VMEM = pl.BlockSpec(memory_space=pltpu.VMEM)


def sds(shape, dtype):
    return jax.ShapeDtypeStruct(shape, dtype)


def call(kernel, out_shape, scratch=(), flops=0, moved=0, transcendentals=0, vmem=24):
    def run(*args):
        return pl.pallas_call(
            kernel,
            out_shape=out_shape,
            in_specs=[VMEM] * len(args),
            out_specs=jax.tree.map(lambda _: VMEM, out_shape),
            scratch_shapes=list(scratch),
            cost_estimate=pl.CostEstimate(
                flops=flops, bytes_accessed=moved, transcendentals=transcendentals
            ),
            compiler_params=pltpu.CompilerParams(vmem_limit_bytes=vmem * 1024 * 1024),
        )(*args)

    return run


class Layout:
    def __init__(self, lat_count, lon_count, kernel_rows):
        self.lat, self.lon = lat_count, lon_count
        self.half = lon_count // 2
        self.groups = (2, (lat_count // 2) * 2, lon_count // 2)
        devices = lat_count * lon_count
        self.rows = -(-kernel_rows // (devices * 8)) * devices * 8
        sizes = []
        rows = self.rows
        for group in self.groups:
            rows //= group
            sizes.append(rows)
        self.chunks = tuple(sizes)

    def ranks(self):
        lat, lon = lax.axis_index("lat"), lax.axis_index("lon")
        return (lat % 2, (lat // 2) * 2 + lon % 2, lon // 2)

    def device(self, ranks):
        lat = (ranks[1] // 2) * 2 + ranks[0]
        lon = ranks[2] * 2 + ranks[1] % 2
        return lat * self.lon + lon

    def exchange(self, level, step):
        pairs = []
        for first in range(self.groups[0]):
            for second in range(self.groups[1]):
                for third in range(self.groups[2]):
                    here = [first, second, third]
                    there = list(here)
                    there[level] ^= step
                    pairs.append((self.device(here), self.device(there)))
        return pairs

    def source(self, lat, lon, forward, steps):
        north = (lon < self.half) == forward
        beside = lat - 1 if north else lat + 1
        if 0 <= beside < self.lat:
            return beside, (lon + steps) % self.lon
        return lat, (lon + steps + self.half) % self.lon

    def meridian(self, forward, steps):
        pairs = []
        for lat in range(self.lat):
            for lon in range(self.lon):
                from_lat, from_lon = self.source(lat, lon, forward, steps)
                pairs.append((from_lat * self.lon + from_lon, lat * self.lon + lon))
        return pairs

    def zonal(self, steps):
        return [
            (lat * self.lon + (lon + steps) % self.lon, lat * self.lon + lon)
            for lat in range(self.lat)
            for lon in range(self.lon)
        ]


def halo_exchange(place, row_forward, row_backward, columns):
    def send(value, pairs):
        return lax.ppermute(value, AXES, pairs)

    return (
        send(row_forward, place.meridian(True, 0)),
        send(row_backward, place.meridian(False, 0)),
        send(columns, place.zonal(-1)),
        send(columns, place.zonal(1)),
        send(columns, place.meridian(True, -1)),
        send(columns, place.meridian(True, 1)),
        send(columns, place.meridian(False, -1)),
        send(columns, place.meridian(False, 1)),
    )


def lanes(shape):
    return lax.broadcasted_iota(jnp.int32, shape, len(shape) - 1)


def edge_columns(row, index, count, columns):
    width = row.shape[1]
    lane = lanes(row.shape)
    first = pltpu.roll(row, index, 1) if index else row
    last = pltpu.roll(row, (count + index + 1) % width, 1)
    columns = jnp.where(lane == index, first, columns)
    return jnp.where(lane == count + index, last, columns)


def pick(flag, yes, no):
    return jnp.where(flag, yes, no)


def widened(place, row_count, rows, halo, emit):
    forward_row, backward_row, west, east, fw_west, fw_east, bw_west, bw_east = halo
    lat, lon = lax.axis_index("lat"), lax.axis_index("lon")
    near = lon < place.half
    northern = lat == 0
    southern = lat == place.lat - 1

    def load(ref):
        return ref[...].astype(F32)

    west_value, east_value = load(west), load(east)
    width = west_value.shape[1]
    lane = lanes(west_value.shape)
    forward_west, backward_west = load(fw_west), load(bw_west)
    forward_east, backward_east = load(fw_east), load(bw_east)

    def corner(value, is_last, offset, target):
        at_last = pltpu.roll(value, (target - offset - row_count + 1) % width, 1)
        at_first = pltpu.roll(value, (target - offset) % width, 1)
        return pick(is_last, at_last, at_first)

    for position in range(row_count + 2):
        index = position - 1
        if index == -1:
            row = pick(near, load(forward_row), load(backward_row))
            left = corner(
                pick(near, forward_west, backward_west), jnp.logical_not(northern), row_count, 0
            )
            right = corner(
                pick(near, forward_east, backward_east), jnp.logical_not(northern), 0, width - 1
            )
        elif index == row_count:
            row = pick(near, load(backward_row), load(forward_row))
            left = corner(pick(near, backward_west, forward_west), southern, row_count, 0)
            right = corner(pick(near, backward_east, forward_east), southern, 0, width - 1)
        else:
            row = rows(index)
            left = pltpu.roll(west_value, (-row_count - index) % width, 1)
            right = pltpu.roll(east_value, (width - 1 - index) % width, 1)
        emit(
            position,
            jnp.where(lane == 0, left, pltpu.roll(row, 1, 1)),
            row,
            jnp.where(lane == width - 1, right, pltpu.roll(row, width - 1, 1)),
        )


def pack_kernel(place, below, hidden, rows_out, forward_out, backward_out, columns_out, wide):
    channels, row_count, width = below.shape
    size = channels * row_count
    wide[0:size, :] = below[...].astype(F32).reshape(size, width)
    wide[size : 2 * size, :] = hidden[...].astype(F32).reshape(size, width)
    columns = jnp.zeros((2 * channels, width), F32)
    edges = []
    for index in range(row_count):
        row = jnp.concatenate(
            [
                wide[pl.ds(index, channels, stride=row_count), :],
                wide[pl.ds(size + index, channels, stride=row_count), :],
            ],
            axis=0,
        )
        rows_out[index] = row.astype(BF16)
        columns = edge_columns(row, index, row_count, columns)
        if index in (0, row_count - 1):
            edges.append(row)
    near = lax.axis_index("lon") < place.half
    forward_out[...] = pick(near, edges[-1], edges[0]).astype(BF16)
    backward_out[...] = pick(near, edges[0], edges[-1]).astype(BF16)
    columns_out[...] = columns.astype(BF16)


def encode(bias):
    high = bias.astype(BF16).astype(F32)
    return jnp.concatenate([high, bias - high], axis=0).astype(BF16)


def decode(block):
    value = block.astype(F32)
    return value[0:8] + value[8:16]


def gates_kernel(
    place,
    rows_in,
    forward_row,
    backward_row,
    west,
    east,
    fw_west,
    fw_east,
    bw_west,
    bw_east,
    cell_prev,
    weights,
    bias_wide,
    readout_wide,
    target,
    land,
    fire,
    hidden_grad,
    hidden_out,
    cell_out,
    grad_cell_out,
    pre_out,
    forward_out,
    backward_out,
    columns_out,
    send_out,
    keep_out,
    bias_out,
    shifted,
    hidden_wide,
    grad_wide,
    sums,
):
    row_count, channels, width = rows_in.shape
    gate_count = weights.shape[1]
    hid = gate_count // 4
    halo = (forward_row, backward_row, west, east, fw_west, fw_east, bw_west, bw_east)

    def emit(position, left, row, right):
        at = pl.ds(position * width, width)
        shifted[0:channels, at] = left.astype(BF16)
        shifted[channels : 2 * channels, at] = row.astype(BF16)
        shifted[2 * channels : 3 * channels, at] = right.astype(BF16)

    widened(place, row_count, lambda index: rows_in[index].astype(F32), halo, emit)
    grad_wide[...] = hidden_grad[...].astype(F32).reshape(hid * row_count, width)

    taps = [
        jnp.concatenate([weights[3 * a], weights[3 * a + 1], weights[3 * a + 2]], axis=1)
        for a in range(3)
    ]
    bias_total = jnp.zeros((gate_count, width), F32)
    columns = jnp.zeros((gate_count, width), F32)
    edges = []
    readout = readout_wide[...]
    pair = 2 if row_count % 2 == 0 else 1
    for base in range(0, row_count, pair):
        preact = jnp.zeros((gate_count, pair * width), F32)
        for a in range(3):
            preact += jnp.dot(
                taps[a],
                shifted[:, pl.ds((base + a) * width, pair * width)],
                preferred_element_type=F32,
            )
        for offset in range(pair):
            index = base + offset
            strided = pl.ds(index, hid, stride=row_count)
            part = preact[:, offset * width : (offset + 1) * width] + bias_wide[...]
            input_gate = 0.5 + 0.5 * jnp.tanh(0.5 * part[0:hid])
            forget_gate = 0.5 + 0.5 * jnp.tanh(0.5 * part[hid : 2 * hid])
            output_gate = 0.5 + 0.5 * jnp.tanh(0.5 * part[2 * hid : 3 * hid])
            candidate = jnp.tanh(part[3 * hid : 4 * hid])
            cell_before = cell_prev[strided, :]
            land_row = land[index : index + 1, :].astype(F32)
            fire_row = fire[index : index + 1, :].astype(F32)
            cell_next = land_row * (forget_gate * cell_before + input_gate * candidate)
            squashed = jnp.tanh(cell_next)
            hidden_next = (output_gate * squashed).astype(BF16).astype(F32)
            predicted = jnp.sum(readout * hidden_next, axis=0, keepdims=True)
            miss = 2.0 * (fire_row * (predicted - target[index : index + 1, :]))
            total_grad = grad_wide[strided, :] + miss * readout
            cell_grad = land_row * total_grad * output_gate * (1.0 - squashed * squashed)
            cell_out[strided, :] = cell_next
            hidden_wide[strided, :] = hidden_next
            grad_cell_out[strided, :] = cell_grad * forget_gate
            pre_grad = jnp.concatenate(
                [
                    cell_grad * candidate * input_gate * (1.0 - input_gate),
                    cell_grad * cell_before * forget_gate * (1.0 - forget_gate),
                    total_grad * squashed * output_gate * (1.0 - output_gate),
                    cell_grad * input_gate * (1.0 - candidate * candidate),
                ],
                axis=0,
            )
            bias_total += pre_grad
            columns = edge_columns(pre_grad, index, row_count, columns)
            pre_out[:, pl.ds(index * width, width)] = pre_grad.astype(BF16)
            if index in (0, row_count - 1):
                edges.append(pre_grad)
    hidden_out[...] = hidden_wide[...].reshape(hidden_out.shape).astype(BF16)
    near = lax.axis_index("lon") < place.half
    forward_out[...] = pick(near, edges[-1], edges[0]).astype(BF16)
    backward_out[...] = pick(near, edges[0], edges[-1]).astype(BF16)
    columns_out[...] = columns.astype(BF16)

    across = (((1,), (1,)), ((), ()))
    for a in range(3):
        product = lax.dot_general(
            pre_out[...],
            shifted[:, pl.ds(a * width, row_count * width)],
            across,
            preferred_element_type=F32,
        )
        for b in range(3):
            at = (3 * a + b) * gate_count
            sums[at : at + gate_count, :] = product[:, b * channels : (b + 1) * channels]
    used = 9 * gate_count
    if place.rows > used:
        sums[used:, :] = jnp.zeros((place.rows - used, channels), F32)

    ones = jnp.ones((8, width), BF16)
    high = bias_total.astype(BF16)
    low = (bias_total - high.astype(F32)).astype(BF16)
    flat = lax.dot_general(ones, high, across, preferred_element_type=F32)
    flat += lax.dot_general(ones, low, across, preferred_element_type=F32)
    odd = lax.broadcasted_iota(jnp.int32, (8, channels), 0) % 2 == 1
    bias_rows = jnp.where(odd, flat[:, channels : 2 * channels], flat[:, 0:channels])
    bias_out[...] = bias_rows

    rank = place.ranks()[0]
    chunk = place.chunks[0]
    send_out[0:BIAS_ROWS, :] = encode(bias_rows)
    send_out[BIAS_ROWS:, :] = sums[pl.ds(pl.multiple_of((1 - rank) * chunk, 8), chunk), :].astype(
        BF16
    )
    keep_out[...] = sums[pl.ds(pl.multiple_of(rank * chunk, 8), chunk), :]


def reduce_kernel(place, level, scaling, *refs):
    arrived = place.groups[level] - 1
    keep, bias = refs[0], refs[1]
    received = refs[2 : 2 + arrived]
    outs = refs[2 + arrived :]
    total = keep[...]
    bias_total = bias[...]
    for ref in received:
        total += ref[BIAS_ROWS:, :].astype(F32)
        bias_total += decode(ref[0:BIAS_ROWS, :])
    if level == len(place.groups) - 1:
        outs[0][0:BIAS_ROWS, :] = encode(bias_total * scaling)
        outs[0][BIAS_ROWS:, :] = (total * scaling).astype(BF16)
        return
    group, chunk = place.groups[level + 1], place.chunks[level + 1]
    sends = outs[: group - 1]
    keep_out, bias_out, scratch = outs[group - 1 :]
    scratch[...] = total
    rank = place.ranks()[level + 1]
    block = encode(bias_total)
    for step, send in enumerate(sends, 1):
        at = pl.ds(pl.multiple_of((rank ^ step) * chunk, 8), chunk)
        send[0:BIAS_ROWS, :] = block
        send[BIAS_ROWS:, :] = scratch[at, :].astype(BF16)
    keep_out[...] = scratch[pl.ds(pl.multiple_of(rank * chunk, 8), chunk), :]
    bias_out[...] = bias_total


def choose(rank, blocks):
    chosen = blocks[0]
    for step in range(1, len(blocks)):
        chosen = pick(rank == step, blocks[step], chosen)
    return chosen


def gather_kernel(place, level, *refs):
    blocks, out, scratch = refs[:-2], refs[-2], refs[-1]
    rank = place.ranks()[level]
    chunk = blocks[0].shape[0] - BIAS_ROWS
    bias = choose(rank, [block[0:BIAS_ROWS, :].astype(F32) for block in blocks])
    for step, block in enumerate(blocks):
        scratch[step * chunk : (step + 1) * chunk, :] = block[BIAS_ROWS:, :].astype(F32)
    out[0:BIAS_ROWS, :] = bias.astype(BF16)
    out[BIAS_ROWS:, :] = scratch[...].astype(BF16)


def place_kernel(place, *refs):
    blocks, out, bias_out, scratch = refs[:-3], refs[-3], refs[-2], refs[-1]
    ranks = place.ranks()
    middle, last = place.groups[1], place.groups[2]
    chunk = place.chunks[2]
    biases = []
    for first in range(2):
        part = blocks[first * middle : (first + 1) * middle]
        biases.append(
            choose(ranks[1], [block[0:BIAS_ROWS, :].astype(F32) for block in part])
        )
        for second in range(middle):
            scratch[...] = part[second][BIAS_ROWS:, :].astype(F32)
            base = (ranks[0] ^ first) * place.chunks[0] + (ranks[1] ^ second) * place.chunks[1]
            for third in range(last):
                at = pl.multiple_of(base + (ranks[2] ^ third) * chunk, 8)
                out[pl.ds(at, chunk), :] = scratch[third * chunk : (third + 1) * chunk, :]
    bias_out[...] = decode(choose(ranks[0], biases))


def field_kernel(
    place,
    pre,
    forward_row,
    backward_row,
    west,
    east,
    fw_west,
    fw_east,
    bw_west,
    bw_east,
    weights,
    inputs_out,
    hidden_out,
    shifted,
    turned,
    wide,
):
    gate_count, cells = pre.shape
    channels = weights.shape[2]
    hid, row_count, width = hidden_out.shape
    halo = (forward_row, backward_row, west, east, fw_west, fw_east, bw_west, bw_east)

    def emit(position, left, row, right):
        at = pl.ds(position * width, width)
        shifted[0:gate_count, at] = right.astype(BF16)
        shifted[gate_count : 2 * gate_count, at] = row.astype(BF16)
        shifted[2 * gate_count : 3 * gate_count, at] = left.astype(BF16)

    widened(
        place,
        row_count,
        lambda index: pre[:, pl.ds(index * width, width)].astype(F32),
        halo,
        emit,
    )
    for a in range(3):
        for b in range(3):
            turned[a, :, b * gate_count : (b + 1) * gate_count] = weights[3 * a + b].T
    northern = lax.axis_index("lat") == 0
    southern = lax.axis_index("lat") == place.lat - 1
    top = turned[jnp.where(northern, 0, 2)]
    bottom = turned[jnp.where(southern, 2, 0)]

    def product(matrix, position, count):
        return jnp.dot(
            matrix, shifted[:, pl.ds(position * width, count * width)], preferred_element_type=F32
        )

    pair = 2 if row_count % 2 == 0 else 1
    for base in range(0, row_count, pair):
        total = product(turned[1], base + 1, pair)
        if base == 0:
            above = product(top, 0, 1)
            if pair == 2:
                above = jnp.concatenate([above, product(turned[2], 1, 1)], axis=1)
        else:
            above = product(turned[2], base, pair)
        if base + pair == row_count:
            below = product(bottom, row_count + 1, 1)
            if pair == 2:
                below = jnp.concatenate([product(turned[0], row_count, 1), below], axis=1)
        else:
            below = product(turned[0], base + 2, pair)
        total = total + above + below
        for offset in range(pair):
            value = total[:, offset * width : (offset + 1) * width]
            index = base + offset
            wide[pl.ds(index, channels, stride=row_count), :] = value
    size = (channels - hid) * row_count
    inputs_out[...] = wide[0:size, :].reshape(inputs_out.shape).astype(BF16)
    hidden_out[...] = wide[size:, :].reshape(hidden_out.shape).astype(BF16)


def body(
    place,
    inputs_below,
    hidden_prev,
    cell_prev,
    kernel_weights,
    gate_bias,
    readout,
    target_field,
    land_mask,
    fire_mask,
    hidden_grad,
):
    hid, row_count, width = hidden_prev.shape
    gate_count, channels = kernel_weights.shape[1:]
    cells = row_count * width
    halo_cells = (row_count + 2) * width
    scaling = 1.0 / math.sqrt(cells * place.lat * place.lon)
    bind = functools.partial

    packed, forward, backward, columns = call(
        bind(pack_kernel, place),
        (
            sds((row_count, channels, width), BF16),
            sds((channels, width), BF16),
            sds((channels, width), BF16),
            sds((channels, width), BF16),
        ),
        [pltpu.VMEM((channels * row_count, width), F32)],
        moved=4 * channels * cells,
    )(inputs_below, hidden_prev)
    halo = halo_exchange(place, forward, backward, columns)

    chunks, groups = place.chunks, place.groups
    (
        hidden_next,
        cell_next,
        grad_cell,
        pre,
        pre_forward,
        pre_backward,
        pre_columns,
        send,
        keep,
        bias,
    ) = call(
        bind(gates_kernel, place),
        (
            sds((hid, row_count, width), BF16),
            sds((hid * row_count, width), F32),
            sds((hid * row_count, width), F32),
            sds((gate_count, cells), BF16),
            sds((gate_count, width), BF16),
            sds((gate_count, width), BF16),
            sds((gate_count, width), BF16),
            sds((BIAS_ROWS + chunks[0], channels), BF16),
            sds((chunks[0], channels), F32),
            sds((8, channels), F32),
        ),
        [
            pltpu.VMEM((3 * channels, halo_cells), BF16),
            pltpu.VMEM((hid * row_count, width), F32),
            pltpu.VMEM((hid * row_count, width), F32),
            pltpu.VMEM((place.rows, channels), F32),
        ],
        flops=4 * 9 * gate_count * channels * cells,
        moved=4_000_000,
        transcendentals=5 * hid * cells,
    )(
        packed,
        *halo,
        cell_prev.reshape(hid * row_count, width),
        kernel_weights,
        jnp.broadcast_to(gate_bias[:, None], (gate_count, width)),
        jnp.broadcast_to(readout[:, None], (hid, width)),
        target_field,
        land_mask,
        fire_mask,
        hidden_grad,
    )

    def swap(value, level, step):
        return lax.ppermute(value, AXES, place.exchange(level, step))

    sends = [send]
    pre_halo = None
    for level in range(3):
        received = [swap(block, level, step) for step, block in enumerate(sends, 1)]
        if level == 0:
            pre_halo = halo_exchange(place, pre_forward, pre_backward, pre_columns)
        if level < 2:
            outs = [sds((BIAS_ROWS + chunks[level + 1], channels), BF16)] * (groups[level + 1] - 1)
            outs += [sds((chunks[level + 1], channels), F32), sds((8, channels), F32)]
            scratch = [pltpu.VMEM((chunks[level], channels), F32)]
        else:
            outs = [sds((BIAS_ROWS + chunks[2], channels), BF16)]
            scratch = []
        results = call(
            bind(reduce_kernel, place, level, scaling),
            tuple(outs),
            scratch,
            moved=8 * chunks[level] * channels,
        )(keep, bias, *received)
        if level < 2:
            sends, keep, bias = results[:-2], results[-2], results[-1]
    block = results[0]

    grad_inputs, grad_hidden = call(
        bind(field_kernel, place),
        (sds((channels - hid, row_count, width), BF16), sds((hid, row_count, width), BF16)),
        [
            pltpu.VMEM((3 * gate_count, halo_cells), BF16),
            pltpu.VMEM((3, channels, 3 * gate_count), BF16),
            pltpu.VMEM((channels * row_count, width), F32),
        ],
        flops=2 * 9 * gate_count * channels * cells,
        moved=2_000_000,
    )(pre, *pre_halo, kernel_weights)

    blocks = [block] + [swap(block, 2, step) for step in range(1, groups[2])]
    joined = call(
        bind(gather_kernel, place, 2),
        sds((BIAS_ROWS + chunks[1], channels), BF16),
        [pltpu.VMEM((chunks[1], channels), F32)],
        moved=4 * chunks[1] * channels,
    )(*blocks)
    parts = [joined] + [swap(joined, 1, step) for step in range(1, groups[1])]
    parts += [swap(part, 0, 1) for part in parts]
    grad_kernel, grad_bias = call(
        bind(place_kernel, place),
        (sds((place.rows, channels), F32), sds((8, channels), F32)),
        [pltpu.VMEM((chunks[1], channels), F32)],
        moved=6 * place.rows * channels,
    )(*parts)
    shape = hidden_prev.shape
    return (
        hidden_next,
        cell_next.reshape(shape),
        grad_inputs,
        grad_hidden,
        grad_cell.reshape(shape),
        grad_kernel[: 9 * gate_count].reshape(kernel_weights.shape),
        grad_bias[: gate_count // channels].reshape(gate_count),
    )


def solution(mesh):
    field = P(None, "lat", "lon")
    flat = P("lat", "lon")

    def run(*args):
        place = Layout(
            mesh.shape["lat"], mesh.shape["lon"], args[3].shape[0] * args[3].shape[1]
        )
        return jax.shard_map(
            functools.partial(body, place),
            mesh=mesh,
            in_specs=(field, field, field, P(), P(), P(), flat, flat, flat, field),
            out_specs=(field, field, field, field, field, P(), P()),
            check_vma=False,
        )(*args)

    return run
```

time: 250 us -> 81.5 us (0.33)
  waiting for transfers between devices: 126 us -> 20.8 us
  blocking collectives: 43.5 us -> 0 us
  starting transfers between devices: 20.7 us -> 44.5 us
  other arithmetic: 17.8 us -> 0 us
  between operations: 14.4 us -> 0.78 us
  local copies, waits for them, and re-layouts: 21.4 us -> 8.84 us
  Pallas kernels: 0 us -> 6.2 us
  matrix products: 6.02 us -> 0 us
    psum x1 -> x0, waiting for transfers between devices: 114 us -> none  [body(): lax.psum((local_kernel, local_bias), ('lat', 'lon'))]
    psum x1 -> x0, blocking collectives: 43.5 us -> none  [body(): lax.psum((local_kernel, local_bias), ('lat', 'lon'))]
    ppermute x10 -> x33, starting transfers between devices: 20.7 us -> 44.5 us  [the longest x16 26.1 us: send(): return lax.ppermute(value, AXES, pairs)]
    ppermute x10 -> x33, waiting for transfers between devices: 11.3 us -> 20.8 us  [the longest x16 11.6 us: send(): return lax.ppermute(value, AXES, pairs)]
    pallas_call x0 -> x8, Pallas kernels: none -> 6.2 us  [run(): pl.pallas_call(kernel, out_shape=out_shape, in_specs=[VMEM] * len(args),...]
    dot_general x9 -> x0, matrix products: 6.02 us -> none  [the longest x1 2.05 us: body(): jnp.einsum('grw,krw->gk', pre_low, patches, preferred_element_type=jnp.fl...]
    concatenate x8 -> x0, other arithmetic: 5.53 us -> none  [the longest x2 1.86 us: with_halo(): jnp.concatenate([lax.ppermute(tail, axis, [(i, (i + 1) % count) for i in...]
    slice x6 -> x0, local copies, waits for them, and re-layouts: 4.31 us -> none  [the longest x2 1.38 us: with_halo(): lax.slice_in_dim(cells, cells.shape[dim] - width, cells.shape[dim], axis=...]
  transfers between devices with their start and end apart: 11 -> 33, of which waited for: 5 -> 13; matrix products, arithmetic and copies ran while one was open for 9% -> 0% of each run, Pallas kernels for 0% -> 3%
where the time goes in v1:
time: 81.5 us; the launch traced here: 81.2 us
  starting transfers between devices  44.5 us (55%)
  waiting for transfers between devices  20.8 us (26%)
  local copies, waits for them, and re-layouts  8.84 us (11%)
  Pallas kernels  6.2 us (8%)
    ppermute x16, starting transfers between devices, send(): return lax.ppermute(value, AXES, pairs)  26.1 us
    ppermute x17, starting transfers between devices, swap(): return lax.ppermute(value, AXES, place.exchange(level, step))  18.4 us
    ppermute x16, waiting for transfers between devices, send(): return lax.ppermute(value, AXES, pairs)  11.6 us
    ppermute x17, waiting for transfers between devices, swap(): return lax.ppermute(value, AXES, place.exchange(level, step))  9.19 us
    unnamed x18, local copies, waits for them, and re-layouts  6.78 us
    pallas_call x8, Pallas kernels, run(): pl.pallas_call(kernel, out_shape=out_shape, in_specs=[VMEM] * len(args),...  6.2 us
  transfers between devices with their start and end apart: 33, of which 13 were waited for; matrix products, arithmetic and copies ran while one was open for 0% of the time, Pallas kernels for 3%

profile of v1, /device:TPU:0, one launch (start us, length us, event | category | flops | bytes accessed | tf_op | source)
XLA Modules:
  0.0 81.2 jit_solution(18290313653360098747)
XLA Ops:
  0.6 0.9 %copy-done = bf16[64,8,128]{2,1,0:T(8,128)(2,1)S(1)} copy-done((bf16[64,8,128]{2,1,0:T(8,128)(2,1)S(1)}, bf16[64,8,128]{2,1,0:T(8,128)(2,1)}, u32[]{:S(2)}) %copy-start) | copy-done | bytes 131096
  1.5 0.9 %copy-done.1 = bf16[64,8,128]{2,1,0:T(8,128)(2,1)S(1)} copy-done((bf16[64,8,128]{2,1,0:T(8,128)(2,1)S(1)}, bf16[64,8,128]{2,1,0:T(8,128)(2,1)}, u32[]{:S(2)}) %copy-start.1) | copy-done | bytes 131096
  2.4 0.3 shard_map.153
  2.7 0.5 collective-permute-start
  3.2 3.7 %collective-permute-start.1 = (bf16[128,128]{1,0:T(8,128)(2,1)S(1)}, bf16[128,128]{1,0:T(8,128)(2,1)S(1)}, u32[]{:S(2)}, u32[]{:S(2)}) collective-permute-start(bf16[128,128]{1,0:T(8,128)(2,1)S(1)} %get-tuple-element.37), channel_id=1, source_target_pairs={{8,0},{9,1},{10,2},{11,3},{0,4},{1,5},{2,6},{3,7},{16,8},{17,9},{1... | collective-permute-start | bytes 98312 | tf_op jit(solution)/shard_map/ppermute | solution.py:98
  6.9 3.2 %collective-permute-start.7 = (bf16[128,128]{1,0:T(8,128)(2,1)S(1)}, bf16[128,128]{1,0:T(8,128)(2,1)S(1)}, u32[]{:S(2)}, u32[]{:S(2)}) collective-permute-start(bf16[128,128]{1,0:T(8,128)(2,1)S(1)} %get-tuple-element.38), channel_id=1, source_target_pairs={{9,0},{10,1},{11,2},{12,3},{1,4},{2,5},{3,6},{4,7},{17,8},{18,9},{... | collective-permute-start | bytes 98312 | tf_op jit(solution)/shard_map/ppermute | solution.py:98
  10.1 2.3 %collective-permute-start.5 = (bf16[128,128]{1,0:T(8,128)(2,1)S(1)}, bf16[128,128]{1,0:T(8,128)(2,1)S(1)}, u32[]{:S(2)}, u32[]{:S(2)}) collective-permute-start(bf16[128,128]{1,0:T(8,128)(2,1)S(1)} %get-tuple-element.38), channel_id=1, source_target_pairs={{5,0},{6,1},{7,2},{0,3},{13,4},{14,5},{15,6},{8,7},{1,8},{2,9},{3,... | collective-permute-start | bytes 98312 | tf_op jit(solution)/shard_map/ppermute | solution.py:98
  12.3 0.9 %collective-permute-start.4 = (bf16[128,128]{1,0:T(8,128)(2,1)S(1)}, bf16[128,128]{1,0:T(8,128)(2,1)S(1)}, u32[]{:S(2)}, u32[]{:S(2)}) collective-permute-start(bf16[128,128]{1,0:T(8,128)(2,1)S(1)} %get-tuple-element.38), channel_id=1, source_target_pairs={{3,0},{4,1},{5,2},{6,3},{11,4},{12,5},{13,6},{14,7},{7,8},{0,9},{1... | collective-permute-start | bytes 98312 | tf_op jit(solution)/shard_map/ppermute | solution.py:98
  13.3 3.4 %collective-permute-start.3 = (bf16[128,128]{1,0:T(8,128)(2,1)S(1)}, bf16[128,128]{1,0:T(8,128)(2,1)S(1)}, u32[]{:S(2)}, u32[]{:S(2)}) collective-permute-start(bf16[128,128]{1,0:T(8,128)(2,1)S(1)} %get-tuple-element.38), channel_id=1, source_target_pairs={{1,0},{2,1},{3,2},{4,3},{5,4},{6,5},{7,6},{0,7},{9,8},{10,9},{11,1... | collective-permute-start | bytes 98312 | tf_op jit(solution)/shard_map/ppermute | solution.py:98
  16.7 0.5 collective-permute-done.4.fw_west
  17.2 1.0 %collective-permute-done.3.east = bf16[128,128]{1,0:T(8,128)(2,1)S(1)} collective-permute-done((bf16[128,128]{1,0:T(8,128)(2,1)S(1)}, bf16[128,128]{1,0:T(8,128)(2,1)S(1)}, u32[]{:S(2)}, u32[]{:S(2)}) %collective-permute-start.3) | collective-permute-done | bytes 32800 | tf_op jit(solution)/shard_map/ppermute | solution.py:98
  18.3 5.0 %collective-permute-done.2.west = bf16[128,128]{1,0:T(8,128)(2,1)S(1)} collective-permute-done((bf16[128,128]{1,0:T(8,128)(2,1)S(1)}, bf16[128,128]{1,0:T(8,128)(2,1)S(1)}, u32[]{:S(2)}, u32[]{:S(2)}) %collective-permute-start.2) | collective-permute-done | bytes 32800 | tf_op jit(solution)/shard_map/ppermute | solution.py:98
  23.3 0.7 broadcast_in_dim.5.readout_wide
  24.0 0.8 broadcast_in_dim.4.bias_wide
  24.8 1.1 %copy-done.2 = bf16[9,256,128]{2,1,0:T(8,128)(2,1)S(1)} copy-done((bf16[9,256,128]{2,1,0:T(8,128)(2,1)S(1)}, bf16[9,256,128]{2,1,0:T(8,128)(2,1)}, u32[]{:S(2)}) %copy-start.2) | copy-done | bytes 589848
  25.8 0.9 %copy-done.4 = f32[64,8,128]{2,1,0:T(8,128)S(1)} copy-done((f32[64,8,128]{2,1,0:T(8,128)S(1)}, f32[64,8,128]{2,1,0:T(8,128)}, u32[]{:S(2)}) %copy-start.4) | copy-done | bytes 262168
  26.8 0.9 %copy-done.5 = bf16[64,8,128]{2,1,0:T(8,128)(2,1)S(1)} copy-done((bf16[64,8,128]{2,1,0:T(8,128)(2,1)S(1)}, bf16[64,8,128]{2,1,0:T(8,128)(2,1)}, u32[]{:S(2)}) %copy-start.5) | copy-done | bytes 131096
  27.7 0.7 copy-done.6
  28.4 0.7 copy-done.7
  29.1 0.7 copy-done.8
  29.8 2.5 %shard_map.154 = (bf16[64,8,128]{2,1,0:T(8,128)(2,1)}, f32[512,128]{1,0:T(8,128)}, f32[512,128]{1,0:T(8,128)}, bf16[256,1024]{1,0:T(8,128)(2,1)S(1)}, bf16[256,1...) custom-call(bf16[8,128,128]{2,1,0:T(8,128)(2,1)S(1)} %get-tuple-elem, ...), custom_call_target="tpu_custom_call" | custom-call | flops 1207959552 | bytes 4000000 | tf_op jit(solution)/shard_map/pallas_call | solution.py:24
  32.3 2.2 %collective-permute-start.16 = (bf16[1168,128]{1,0:T(8,128)(2,1)S(1)}, bf16[1168,128]{1,0:T(8,128)(2,1)S(1)}, u32[]{:S(2)}, u32[]{:S(2)}) collective-permute-start(bf16[1168,128]{1,0:T(8,128)(2,1)S(1)} %get-tuple-element.50), channel_id=1, source_target_pairs={{0,8},{2,10},{4,12},{6,14},{1,9},{3,11},{5,13},{7,15},{16,24},{18,... | collective-permute-start | bytes 897032 | tf_op jit(solution)/shard_map/ppermute | solution.py:572
  34.5 1.2 %collective-permute-done.16.refs_2_ = bf16[1168,128]{1,0:T(8,128)(2,1)S(1)} collective-permute-done((bf16[1168,128]{1,0:T(8,128)(2,1)S(1)}, bf16[1168,128]{1,0:T(8,128)(2,1)S(1)}, u32[]{:S(2)}, u32[]{:S(2)}) %collective-permute-start.16) | collective-permute-done | bytes 299040 | tf_op jit(solution)/shard_map/ppermute | solution.py:572
  35.9 2.2 %collective-permute-start.18 = (bf16[304,128]{1,0:T(8,128)(2,1)S(1)}, bf16[304,128]{1,0:T(8,128)(2,1)S(1)}, u32[]{:S(2)}, u32[]{:S(2)}) collective-permute-start(bf16[304,128]{1,0:T(8,128)(2,1)S(1)} %get-tuple-element.54), channel_id=1, source_target_pairs={{0,16},{2,18},{4,20},{6,22},{1,17},{3,19},{5,21},{7,23},{16,0},{18... | collective-permute-start | bytes 233480 | tf_op jit(solution)/shard_map/ppermute | solution.py:572
  38.1 1.4 %collective-permute-start.19 = (bf16[304,128]{1,0:T(8,128)(2,1)S(1)}, bf16[304,128]{1,0:T(8,128)(2,1)S(1)}, u32[]{:S(2)}, u32[]{:S(2)}) collective-permute-start(bf16[304,128]{1,0:T(8,128)(2,1)S(1)} %get-tuple-element.55), channel_id=1, source_target_pairs={{0,17},{2,19},{4,21},{6,23},{1,16},{3,18},{5,20},{7,22},{16,1},{18... | collective-permute-start | bytes 233480 | tf_op jit(solution)/shard_map/ppermute | solution.py:572
  39.5 1.0 %collective-permute-done.17.refs_2_ = bf16[304,128]{1,0:T(8,128)(2,1)S(1)} collective-permute-done((bf16[304,128]{1,0:T(8,128)(2,1)S(1)}, bf16[304,128]{1,0:T(8,128)(2,1)S(1)}, u32[]{:S(2)}, u32[]{:S(2)}) %collective-permute-start.17) | collective-permute-done | bytes 77856 | tf_op jit(solution)/shard_map/ppermute | solution.py:572
  40.7 2.8 %collective-permute-done.19.refs_4_ = bf16[304,128]{1,0:T(8,128)(2,1)S(1)} collective-permute-done((bf16[304,128]{1,0:T(8,128)(2,1)S(1)}, bf16[304,128]{1,0:T(8,128)(2,1)S(1)}, u32[]{:S(2)}, u32[]{:S(2)}) %collective-permute-start.19) | collective-permute-done | bytes 77856 | tf_op jit(solution)/shard_map/ppermute | solution.py:572
  43.6 0.9 %collective-permute-start.21 = (bf16[88,128]{1,0:T(8,128)(2,1)S(1)}, bf16[88,128]{1,0:T(8,128)(2,1)S(1)}, u32[]{:S(2)}, u32[]{:S(2)}) collective-permute-start(bf16[88,128]{1,0:T(8,128)(2,1)S(1)} %get-tuple-element.59), channel_id=1, source_target_pairs={{0,4},{2,6},{4,0},{6,2},{1,5},{3,7},{5,1},{7,3},{16,20},{18,22},{2... | collective-permute-start | bytes 67592 | tf_op jit(solution)/shard_map/ppermute | solution.py:572
  44.6 3.5 %collective-permute-start.22 = (bf16[88,128]{1,0:T(8,128)(2,1)S(1)}, bf16[88,128]{1,0:T(8,128)(2,1)S(1)}, u32[]{:S(2)}, u32[]{:S(2)}) collective-permute-start(bf16[88,128]{1,0:T(8,128)(2,1)S(1)} %get-tuple-element.60), channel_id=1, source_target_pairs={{0,6},{2,4},{4,2},{6,0},{1,7},{3,5},{5,3},{7,1},{16,22},{18,20},{2... | collective-permute-start | bytes 67592 | tf_op jit(solution)/shard_map/ppermute | solution.py:572
  48.0 0.4 collective-permute-done.21.refs_3_
  48.4 1.7 %collective-permute-done.22.refs_4_ = bf16[88,128]{1,0:T(8,128)(2,1)S(1)} collective-permute-done((bf16[88,128]{1,0:T(8,128)(2,1)S(1)}, bf16[88,128]{1,0:T(8,128)(2,1)S(1)}, u32[]{:S(2)}, u32[]{:S(2)}) %collective-permute-start.22) | collective-permute-done | bytes 22560 | tf_op jit(solution)/shard_map/ppermute | solution.py:572
  50.2 3.5 %collective-permute-start.25 = (bf16[88,128]{1,0:T(8,128)(2,1)S(1)}, bf16[88,128]{1,0:T(8,128)(2,1)S(1)}, u32[]{:S(2)}, u32[]{:S(2)}) collective-permute-start(bf16[88,128]{1,0:T(8,128)(2,1)S(1)} %shard_map.158.refs_0_), channel_id=1, source_target_pairs={{0,6},{2,4},{4,2},{6,0},{1,7},{3,5},{5,3},{7,1},{16,22},{18,20},{2... | collective-permute-start | bytes 67592 | tf_op jit(solution)/shard_map/ppermute | solution.py:572
  53.7 2.9 %collective-permute-start.9 = (bf16[256,128]{1,0:T(8,128)(2,1)S(1)}, bf16[256,128]{1,0:T(8,128)(2,1)S(1)}, u32[]{:S(2)}, u32[]{:S(2)}) collective-permute-start(bf16[256,128]{1,0:T(8,128)(2,1)S(1)} %get-tuple-element.43), channel_id=1, source_target_pairs={{8,0},{9,1},{10,2},{11,3},{0,4},{1,5},{2,6},{3,7},{16,8},{17,9},{1... | collective-permute-start | bytes 196616 | tf_op jit(solution)/shard_map/ppermute | solution.py:98
  56.6 3.6 %collective-permute-start.14 = (bf16[256,128]{1,0:T(8,128)(2,1)S(1)}, bf16[256,128]{1,0:T(8,128)(2,1)S(1)}, u32[]{:S(2)}, u32[]{:S(2)}) collective-permute-start(bf16[256,128]{1,0:T(8,128)(2,1)S(1)} %get-tuple-element.44), channel_id=1, source_target_pairs={{15,0},{8,1},{9,2},{10,3},{7,4},{0,5},{1,6},{2,7},{23,8},{16,9},{1... | collective-permute-start | bytes 196616 | tf_op jit(solution)/shard_map/ppermute | solution.py:98
  60.3 2.0 %collective-permute-start.13 = (bf16[256,128]{1,0:T(8,128)(2,1)S(1)}, bf16[256,128]{1,0:T(8,128)(2,1)S(1)}, u32[]{:S(2)}, u32[]{:S(2)}) collective-permute-start(bf16[256,128]{1,0:T(8,128)(2,1)S(1)} %get-tuple-element.44), channel_id=1, source_target_pairs={{5,0},{6,1},{7,2},{0,3},{13,4},{14,5},{15,6},{8,7},{1,8},{2,9},{3,... | collective-permute-start | bytes 196616 | tf_op jit(solution)/shard_map/ppermute | solution.py:98
  62.3 1.8 %collective-permute-done.23.refs_1_ = bf16[88,128]{1,0:T(8,128)(2,1)S(1)} collective-permute-done((bf16[88,128]{1,0:T(8,128)(2,1)S(1)}, bf16[88,128]{1,0:T(8,128)(2,1)S(1)}, u32[]{:S(2)}, u32[]{:S(2)}) %collective-permute-start.23) | collective-permute-done | bytes 22560 | tf_op jit(solution)/shard_map/ppermute | solution.py:572
  64.1 1.8 %collective-permute-start.28 = (bf16[304,128]{1,0:T(8,128)(2,1)S(1)}, bf16[304,128]{1,0:T(8,128)(2,1)S(1)}, u32[]{:S(2)}, u32[]{:S(2)}) collective-permute-start(bf16[304,128]{1,0:T(8,128)(2,1)S(1)} %shard_map.159.refs_0_), channel_id=1, source_target_pairs={{0,17},{2,19},{4,21},{6,23},{1,16},{3,18},{5,20},{7,22},{16,1},{18... | collective-permute-start | bytes 233480 | tf_op jit(solution)/shard_map/ppermute | solution.py:572
  65.9 0.4 collective-permute-start.27
  66.3 1.4 %collective-permute-start.26 = (bf16[304,128]{1,0:T(8,128)(2,1)S(1)}, bf16[304,128]{1,0:T(8,128)(2,1)S(1)}, u32[]{:S(2)}, u32[]{:S(2)}) collective-permute-start(bf16[304,128]{1,0:T(8,128)(2,1)S(1)} %shard_map.159.refs_0_), channel_id=1, source_target_pairs={{0,1},{2,3},{4,5},{6,7},{1,0},{3,2},{5,4},{7,6},{16,17},{18,19},{2... | collective-permute-start | bytes 233480 | tf_op jit(solution)/shard_map/ppermute | solution.py:572
  67.7 2.5 %collective-permute-start.11 = (bf16[256,128]{1,0:T(8,128)(2,1)S(1)}, bf16[256,128]{1,0:T(8,128)(2,1)S(1)}, u32[]{:S(2)}, u32[]{:S(2)}) collective-permute-start(bf16[256,128]{1,0:T(8,128)(2,1)S(1)} %get-tuple-element.44), channel_id=1, source_target_pairs={{1,0},{2,1},{3,2},{4,3},{5,4},{6,5},{7,6},{0,7},{9,8},{10,9},{11,1... | collective-permute-start | bytes 196616 | tf_op jit(solution)/shard_map/ppermute | solution.py:98
  70.4 1.1 %collective-permute-start.10 = (bf16[256,128]{1,0:T(8,128)(2,1)S(1)}, bf16[256,128]{1,0:T(8,128)(2,1)S(1)}, u32[]{:S(2)}, u32[]{:S(2)}) collective-permute-start(bf16[256,128]{1,0:T(8,128)(2,1)S(1)} %get-tuple-element.44), channel_id=1, source_target_pairs={{7,0},{0,1},{1,2},{2,3},{3,4},{4,5},{5,6},{6,7},{15,8},{8,9},{9,10... | collective-permute-start | bytes 196616 | tf_op jit(solution)/shard_map/ppermute | solution.py:98
  71.4 2.6 %collective-permute-done.11.east = bf16[256,128]{1,0:T(8,128)(2,1)S(1)} collective-permute-done((bf16[256,128]{1,0:T(8,128)(2,1)S(1)}, bf16[256,128]{1,0:T(8,128)(2,1)S(1)}, u32[]{:S(2)}, u32[]{:S(2)}) %collective-permute-start.11) | collective-permute-done | bytes 65568 | tf_op jit(solution)/shard_map/ppermute | solution.py:98
  74.1 0.4 collective-permute-start.32
  74.6 0.4 collective-permute-start.30
  75.0 2.3 %collective-permute-done.10.west = bf16[256,128]{1,0:T(8,128)(2,1)S(1)} collective-permute-done((bf16[256,128]{1,0:T(8,128)(2,1)S(1)}, bf16[256,128]{1,0:T(8,128)(2,1)S(1)}, u32[]{:S(2)}, u32[]{:S(2)}) %collective-permute-start.10) | collective-permute-done | bytes 65568 | tf_op jit(solution)/shard_map/ppermute | solution.py:98
  77.3 2.1 %shard_map.155 = (bf16[64,8,128]{2,1,0:T(8,128)(2,1)}, bf16[64,8,128]{2,1,0:T(8,128)(2,1)}) custom-call(bf16[256,1024]{1,0:T(8,128)(2,1)S(1)} %get-tuple-element.41.pre, bf16[256,128]{1,0:T(8,128)(2,1)S(1)} %collective-permute-done.8.forward_row, bf16[256,128]{1,0:T(8,128)(2,1)S(1)} %collective-permute-done.9.backward_row, ...), custom_call_target="tpu_custom_call" | custom-call | flops 603979776 | bytes 2000000 | tf_op jit(solution)/shard_map/pallas_call | solution.py:24
  79.5 1.1 %shard_map.160 = (f32[2304,128]{1,0:T(8,128)}, f32[8,128]{1,0:T(8,128)S(1)}) custom-call(bf16[304,128]{1,0:T(8,128)(2,1)S(1)} %shard_map.159.refs_0_, bf16[304,128]{1,0:T(8,128)(2,1)S(1)} %collective-permute-done.26.refs_1_, bf16[304,128]{1,0:T(8,128)(2,1)S(1)} %collective-permute-done.27.refs_2_, bf16[304,128]{1,0:T(8,128)(2,1)S(1)} %collective-permute-done.28.refs_3_, ...), custom_call_target="tpu_custom_call" | custom-call | bytes 1769472 | tf_op jit(solution)/shard_map/pallas_call | solution.py:24
  80.6 0.6 slice_bitcast_fusion
  (47 shorter events, 1.0 us)
Async XLA Ops:
  0.6 0.9 %copy-start = (bf16[64,8,128]{2,1,0:T(8,128)(2,1)S(1)}, bf16[64,8,128]{2,1,0:T(8,128)(2,1)}, u32[]{:S(2)}) copy-start(bf16[64,8,128]{2,1,0:T(8,128)(2,1)} %below.1) | copy-start | bytes 393220
  1.5 0.9 %copy-start.1 = (bf16[64,8,128]{2,1,0:T(8,128)(2,1)S(1)}, bf16[64,8,128]{2,1,0:T(8,128)(2,1)}, u32[]{:S(2)}) copy-start(bf16[64,8,128]{2,1,0:T(8,128)(2,1)} %hidden.1) | copy-start | bytes 393220
  2.7 9.6 %collective-permute-start = (bf16[128,128]{1,0:T(8,128)(2,1)S(1)}, bf16[128,128]{1,0:T(8,128)(2,1)S(1)}, u32[]{:S(2)}, u32[]{:S(2)}) collective-permute-start(bf16[128,128]{1,0:T(8,128)(2,1)S(1)} %get-tuple-element.36), channel_id=1, source_target_pairs={{4,0},{5,1},{6,2},{7,3},{12,4},{13,5},{14,6},{15,7},{0,8},{1,9},{2... | collective-permute-start | bytes 98312 | tf_op jit(solution)/shard_map/ppermute | solution.py:98
  3.2 10.0 %collective-permute-start.1 = (bf16[128,128]{1,0:T(8,128)(2,1)S(1)}, bf16[128,128]{1,0:T(8,128)(2,1)S(1)}, u32[]{:S(2)}, u32[]{:S(2)}) collective-permute-start(bf16[128,128]{1,0:T(8,128)(2,1)S(1)} %get-tuple-element.37), channel_id=1, source_target_pairs={{8,0},{9,1},{10,2},{11,3},{0,4},{1,5},{2,6},{3,7},{16,8},{17,9},{1... | collective-permute-start | bytes 98312 | tf_op jit(solution)/shard_map/ppermute | solution.py:98
  6.9 9.8 %collective-permute-start.7 = (bf16[128,128]{1,0:T(8,128)(2,1)S(1)}, bf16[128,128]{1,0:T(8,128)(2,1)S(1)}, u32[]{:S(2)}, u32[]{:S(2)}) collective-permute-start(bf16[128,128]{1,0:T(8,128)(2,1)S(1)} %get-tuple-element.38), channel_id=1, source_target_pairs={{9,0},{10,1},{11,2},{12,3},{1,4},{2,5},{3,6},{4,7},{17,8},{18,9},{... | collective-permute-start | bytes 98312 | tf_op jit(solution)/shard_map/ppermute | solution.py:98
  10.1 6.6 %collective-permute-start.6 = (bf16[128,128]{1,0:T(8,128)(2,1)S(1)}, bf16[128,128]{1,0:T(8,128)(2,1)S(1)}, u32[]{:S(2)}, u32[]{:S(2)}) collective-permute-start(bf16[128,128]{1,0:T(8,128)(2,1)S(1)} %get-tuple-element.38), channel_id=1, source_target_pairs={{15,0},{8,1},{9,2},{10,3},{7,4},{0,5},{1,6},{2,7},{23,8},{16,9},{1... | collective-permute-start | bytes 98312 | tf_op jit(solution)/shard_map/ppermute | solution.py:98
  10.1 6.6 %collective-permute-start.5 = (bf16[128,128]{1,0:T(8,128)(2,1)S(1)}, bf16[128,128]{1,0:T(8,128)(2,1)S(1)}, u32[]{:S(2)}, u32[]{:S(2)}) collective-permute-start(bf16[128,128]{1,0:T(8,128)(2,1)S(1)} %get-tuple-element.38), channel_id=1, source_target_pairs={{5,0},{6,1},{7,2},{0,3},{13,4},{14,5},{15,6},{8,7},{1,8},{2,9},{3,... | collective-permute-start | bytes 98312 | tf_op jit(solution)/shard_map/ppermute | solution.py:98
  12.3 4.9 %collective-permute-start.4 = (bf16[128,128]{1,0:T(8,128)(2,1)S(1)}, bf16[128,128]{1,0:T(8,128)(2,1)S(1)}, u32[]{:S(2)}, u32[]{:S(2)}) collective-permute-start(bf16[128,128]{1,0:T(8,128)(2,1)S(1)} %get-tuple-element.38), channel_id=1, source_target_pairs={{3,0},{4,1},{5,2},{6,3},{11,4},{12,5},{13,6},{14,7},{7,8},{0,9},{1... | collective-permute-start | bytes 98312 | tf_op jit(solution)/shard_map/ppermute | solution.py:98
  13.3 5.0 %collective-permute-start.3 = (bf16[128,128]{1,0:T(8,128)(2,1)S(1)}, bf16[128,128]{1,0:T(8,128)(2,1)S(1)}, u32[]{:S(2)}, u32[]{:S(2)}) collective-permute-start(bf16[128,128]{1,0:T(8,128)(2,1)S(1)} %get-tuple-element.38), channel_id=1, source_target_pairs={{1,0},{2,1},{3,2},{4,3},{5,4},{6,5},{7,6},{0,7},{9,8},{10,9},{11,1... | collective-permute-start | bytes 98312 | tf_op jit(solution)/shard_map/ppermute | solution.py:98
  16.7 6.6 %collective-permute-start.2 = (bf16[128,128]{1,0:T(8,128)(2,1)S(1)}, bf16[128,128]{1,0:T(8,128)(2,1)S(1)}, u32[]{:S(2)}, u32[]{:S(2)}) collective-permute-start(bf16[128,128]{1,0:T(8,128)(2,1)S(1)} %get-tuple-element.38), channel_id=1, source_target_pairs={{7,0},{0,1},{1,2},{2,3},{3,4},{4,5},{5,6},{6,7},{15,8},{8,9},{9,10... | collective-permute-start | bytes 98312 | tf_op jit(solution)/shard_map/ppermute | solution.py:98
  24.8 1.1 %copy-start.2 = (bf16[9,256,128]{2,1,0:T(8,128)(2,1)S(1)}, bf16[9,256,128]{2,1,0:T(8,128)(2,1)}, u32[]{:S(2)}) copy-start(bf16[9,256,128]{2,1,0:T(8,128)(2,1)} %weights.3) | copy-start | bytes 1769476
  25.8 0.9 %copy-start.4 = (f32[64,8,128]{2,1,0:T(8,128)S(1)}, f32[64,8,128]{2,1,0:T(8,128)}, u32[]{:S(2)}) copy-start(f32[64,8,128]{2,1,0:T(8,128)} %param.12) | copy-start | bytes 786436
  26.8 0.9 %copy-start.5 = (bf16[64,8,128]{2,1,0:T(8,128)(2,1)S(1)}, bf16[64,8,128]{2,1,0:T(8,128)(2,1)}, u32[]{:S(2)}) copy-start(bf16[64,8,128]{2,1,0:T(8,128)(2,1)} %hidden_grad.1) | copy-start | bytes 393220
  27.7 0.7 copy-start.6
  28.4 0.7 copy-start.7
  29.1 0.7 copy-start.8
  32.3 45.1 %copy-start.3 = (bf16[9,256,128]{2,1,0:T(8,128)(2,1)S(1)}, bf16[9,256,128]{2,1,0:T(8,128)(2,1)}, u32[]{:S(2)}) copy-start(bf16[9,256,128]{2,1,0:T(8,128)(2,1)} %weights.3) | copy-start | bytes 1769476
  32.3 3.4 %collective-permute-start.16 = (bf16[1168,128]{1,0:T(8,128)(2,1)S(1)}, bf16[1168,128]{1,0:T(8,128)(2,1)S(1)}, u32[]{:S(2)}, u32[]{:S(2)}) collective-permute-start(bf16[1168,128]{1,0:T(8,128)(2,1)S(1)} %get-tuple-element.50), channel_id=1, source_target_pairs={{0,8},{2,10},{4,12},{6,14},{1,9},{3,11},{5,13},{7,15},{16,24},{18,... | collective-permute-start | bytes 897032 | tf_op jit(solution)/shard_map/ppermute | solution.py:572
  35.8 4.7 %collective-permute-start.17 = (bf16[304,128]{1,0:T(8,128)(2,1)S(1)}, bf16[304,128]{1,0:T(8,128)(2,1)S(1)}, u32[]{:S(2)}, u32[]{:S(2)}) collective-permute-start(bf16[304,128]{1,0:T(8,128)(2,1)S(1)} %get-tuple-element.53), channel_id=1, source_target_pairs={{0,1},{2,3},{4,5},{6,7},{1,0},{3,2},{5,4},{7,6},{16,17},{18,19},{2... | collective-permute-start | bytes 233480 | tf_op jit(solution)/shard_map/ppermute | solution.py:572
  35.9 4.8 %collective-permute-start.18 = (bf16[304,128]{1,0:T(8,128)(2,1)S(1)}, bf16[304,128]{1,0:T(8,128)(2,1)S(1)}, u32[]{:S(2)}, u32[]{:S(2)}) collective-permute-start(bf16[304,128]{1,0:T(8,128)(2,1)S(1)} %get-tuple-element.54), channel_id=1, source_target_pairs={{0,16},{2,18},{4,20},{6,22},{1,17},{3,19},{5,21},{7,23},{16,0},{18... | collective-permute-start | bytes 233480 | tf_op jit(solution)/shard_map/ppermute | solution.py:572
  38.1 5.4 %collective-permute-start.19 = (bf16[304,128]{1,0:T(8,128)(2,1)S(1)}, bf16[304,128]{1,0:T(8,128)(2,1)S(1)}, u32[]{:S(2)}, u32[]{:S(2)}) collective-permute-start(bf16[304,128]{1,0:T(8,128)(2,1)S(1)} %get-tuple-element.55), channel_id=1, source_target_pairs={{0,17},{2,19},{4,21},{6,23},{1,16},{3,18},{5,20},{7,22},{16,1},{18... | collective-permute-start | bytes 233480 | tf_op jit(solution)/shard_map/ppermute | solution.py:572
  39.5 17.2 %collective-permute-start.8 = (bf16[256,128]{1,0:T(8,128)(2,1)S(1)}, bf16[256,128]{1,0:T(8,128)(2,1)S(1)}, u32[]{:S(2)}, u32[]{:S(2)}) collective-permute-start(bf16[256,128]{1,0:T(8,128)(2,1)S(1)} %get-tuple-element.42), channel_id=1, source_target_pairs={{4,0},{5,1},{6,2},{7,3},{12,4},{13,5},{14,6},{15,7},{0,8},{1,9},{2... | collective-permute-start | bytes 196616 | tf_op jit(solution)/shard_map/ppermute | solution.py:98
  43.6 4.5 %collective-permute-start.20 = (bf16[88,128]{1,0:T(8,128)(2,1)S(1)}, bf16[88,128]{1,0:T(8,128)(2,1)S(1)}, u32[]{:S(2)}, u32[]{:S(2)}) collective-permute-start(bf16[88,128]{1,0:T(8,128)(2,1)S(1)} %get-tuple-element.58), channel_id=1, source_target_pairs={{0,2},{2,0},{4,6},{6,4},{1,3},{3,1},{5,7},{7,5},{16,18},{18,16},{2... | collective-permute-start | bytes 67592 | tf_op jit(solution)/shard_map/ppermute | solution.py:572
  43.6 4.8 %collective-permute-start.21 = (bf16[88,128]{1,0:T(8,128)(2,1)S(1)}, bf16[88,128]{1,0:T(8,128)(2,1)S(1)}, u32[]{:S(2)}, u32[]{:S(2)}) collective-permute-start(bf16[88,128]{1,0:T(8,128)(2,1)S(1)} %get-tuple-element.59), channel_id=1, source_target_pairs={{0,4},{2,6},{4,0},{6,2},{1,5},{3,7},{5,1},{7,3},{16,20},{18,22},{2... | collective-permute-start | bytes 67592 | tf_op jit(solution)/shard_map/ppermute | solution.py:572
  44.6 5.6 %collective-permute-start.22 = (bf16[88,128]{1,0:T(8,128)(2,1)S(1)}, bf16[88,128]{1,0:T(8,128)(2,1)S(1)}, u32[]{:S(2)}, u32[]{:S(2)}) collective-permute-start(bf16[88,128]{1,0:T(8,128)(2,1)S(1)} %get-tuple-element.60), channel_id=1, source_target_pairs={{0,6},{2,4},{4,2},{6,0},{1,7},{3,5},{5,3},{7,1},{16,22},{18,20},{2... | collective-permute-start | bytes 67592 | tf_op jit(solution)/shard_map/ppermute | solution.py:572
  50.2 10.1 %collective-permute-start.25 = (bf16[88,128]{1,0:T(8,128)(2,1)S(1)}, bf16[88,128]{1,0:T(8,128)(2,1)S(1)}, u32[]{:S(2)}, u32[]{:S(2)}) collective-permute-start(bf16[88,128]{1,0:T(8,128)(2,1)S(1)} %shard_map.158.refs_0_), channel_id=1, source_target_pairs={{0,6},{2,4},{4,2},{6,0},{1,7},{3,5},{5,3},{7,1},{16,22},{18,20},{2... | collective-permute-start | bytes 67592 | tf_op jit(solution)/shard_map/ppermute | solution.py:572
  53.7 6.6 %collective-permute-start.24 = (bf16[88,128]{1,0:T(8,128)(2,1)S(1)}, bf16[88,128]{1,0:T(8,128)(2,1)S(1)}, u32[]{:S(2)}, u32[]{:S(2)}) collective-permute-start(bf16[88,128]{1,0:T(8,128)(2,1)S(1)} %shard_map.158.refs_0_), channel_id=1, source_target_pairs={{0,4},{2,6},{4,0},{6,2},{1,5},{3,7},{5,1},{7,3},{16,20},{18,22},{2... | collective-permute-start | bytes 67592 | tf_op jit(solution)/shard_map/ppermute | solution.py:572
  53.7 10.4 %collective-permute-start.9 = (bf16[256,128]{1,0:T(8,128)(2,1)S(1)}, bf16[256,128]{1,0:T(8,128)(2,1)S(1)}, u32[]{:S(2)}, u32[]{:S(2)}) collective-permute-start(bf16[256,128]{1,0:T(8,128)(2,1)S(1)} %get-tuple-element.43), channel_id=1, source_target_pairs={{8,0},{9,1},{10,2},{11,3},{0,4},{1,5},{2,6},{3,7},{16,8},{17,9},{1... | collective-permute-start | bytes 196616 | tf_op jit(solution)/shard_map/ppermute | solution.py:98
  56.6 9.3 %collective-permute-start.15 = (bf16[256,128]{1,0:T(8,128)(2,1)S(1)}, bf16[256,128]{1,0:T(8,128)(2,1)S(1)}, u32[]{:S(2)}, u32[]{:S(2)}) collective-permute-start(bf16[256,128]{1,0:T(8,128)(2,1)S(1)} %get-tuple-element.44), channel_id=1, source_target_pairs={{9,0},{10,1},{11,2},{12,3},{1,4},{2,5},{3,6},{4,7},{17,8},{18,9},{... | collective-permute-start | bytes 196616 | tf_op jit(solution)/shard_map/ppermute | solution.py:98
  56.6 9.6 %collective-permute-start.14 = (bf16[256,128]{1,0:T(8,128)(2,1)S(1)}, bf16[256,128]{1,0:T(8,128)(2,1)S(1)}, u32[]{:S(2)}, u32[]{:S(2)}) collective-permute-start(bf16[256,128]{1,0:T(8,128)(2,1)S(1)} %get-tuple-element.44), channel_id=1, source_target_pairs={{15,0},{8,1},{9,2},{10,3},{7,4},{0,5},{1,6},{2,7},{23,8},{16,9},{1... | collective-permute-start | bytes 196616 | tf_op jit(solution)/shard_map/ppermute | solution.py:98
  60.3 3.8 %collective-permute-start.23 = (bf16[88,128]{1,0:T(8,128)(2,1)S(1)}, bf16[88,128]{1,0:T(8,128)(2,1)S(1)}, u32[]{:S(2)}, u32[]{:S(2)}) collective-permute-start(bf16[88,128]{1,0:T(8,128)(2,1)S(1)} %shard_map.158.refs_0_), channel_id=1, source_target_pairs={{0,2},{2,0},{4,6},{6,4},{1,3},{3,1},{5,7},{7,5},{16,18},{18,16},{2... | collective-permute-start | bytes 67592 | tf_op jit(solution)/shard_map/ppermute | solution.py:572
  60.3 7.4 %collective-permute-start.13 = (bf16[256,128]{1,0:T(8,128)(2,1)S(1)}, bf16[256,128]{1,0:T(8,128)(2,1)S(1)}, u32[]{:S(2)}, u32[]{:S(2)}) collective-permute-start(bf16[256,128]{1,0:T(8,128)(2,1)S(1)} %get-tuple-element.44), channel_id=1, source_target_pairs={{5,0},{6,1},{7,2},{0,3},{13,4},{14,5},{15,6},{8,7},{1,8},{2,9},{3,... | collective-permute-start | bytes 196616 | tf_op jit(solution)/shard_map/ppermute | solution.py:98
  64.1 6.3 %collective-permute-start.12 = (bf16[256,128]{1,0:T(8,128)(2,1)S(1)}, bf16[256,128]{1,0:T(8,128)(2,1)S(1)}, u32[]{:S(2)}, u32[]{:S(2)}) collective-permute-start(bf16[256,128]{1,0:T(8,128)(2,1)S(1)} %get-tuple-element.44), channel_id=1, source_target_pairs={{3,0},{4,1},{5,2},{6,3},{11,4},{12,5},{13,6},{14,7},{7,8},{0,9},{1... | collective-permute-start | bytes 196616 | tf_op jit(solution)/shard_map/ppermute | solution.py:98
  64.1 10.0 %collective-permute-start.28 = (bf16[304,128]{1,0:T(8,128)(2,1)S(1)}, bf16[304,128]{1,0:T(8,128)(2,1)S(1)}, u32[]{:S(2)}, u32[]{:S(2)}) collective-permute-start(bf16[304,128]{1,0:T(8,128)(2,1)S(1)} %shard_map.159.refs_0_), channel_id=1, source_target_pairs={{0,17},{2,19},{4,21},{6,23},{1,16},{3,18},{5,20},{7,22},{16,1},{18... | collective-permute-start | bytes 233480 | tf_op jit(solution)/shard_map/ppermute | solution.py:572
  65.9 8.6 %collective-permute-start.27 = (bf16[304,128]{1,0:T(8,128)(2,1)S(1)}, bf16[304,128]{1,0:T(8,128)(2,1)S(1)}, u32[]{:S(2)}, u32[]{:S(2)}) collective-permute-start(bf16[304,128]{1,0:T(8,128)(2,1)S(1)} %shard_map.159.refs_0_), channel_id=1, source_target_pairs={{0,16},{2,18},{4,20},{6,22},{1,17},{3,19},{5,21},{7,23},{16,0},{18... | collective-permute-start | bytes 233480 | tf_op jit(solution)/shard_map/ppermute | solution.py:572
  66.3 8.3 %collective-permute-start.26 = (bf16[304,128]{1,0:T(8,128)(2,1)S(1)}, bf16[304,128]{1,0:T(8,128)(2,1)S(1)}, u32[]{:S(2)}, u32[]{:S(2)}) collective-permute-start(bf16[304,128]{1,0:T(8,128)(2,1)S(1)} %shard_map.159.refs_0_), channel_id=1, source_target_pairs={{0,1},{2,3},{4,5},{6,7},{1,0},{3,2},{5,4},{7,6},{16,17},{18,19},{2... | collective-permute-start | bytes 233480 | tf_op jit(solution)/shard_map/ppermute | solution.py:572
  67.7 6.3 %collective-permute-start.11 = (bf16[256,128]{1,0:T(8,128)(2,1)S(1)}, bf16[256,128]{1,0:T(8,128)(2,1)S(1)}, u32[]{:S(2)}, u32[]{:S(2)}) collective-permute-start(bf16[256,128]{1,0:T(8,128)(2,1)S(1)} %get-tuple-element.44), channel_id=1, source_target_pairs={{1,0},{2,1},{3,2},{4,3},{5,4},{6,5},{7,6},{0,7},{9,8},{10,9},{11,1... | collective-permute-start | bytes 196616 | tf_op jit(solution)/shard_map/ppermute | solution.py:98
  70.4 7.0 %collective-permute-start.10 = (bf16[256,128]{1,0:T(8,128)(2,1)S(1)}, bf16[256,128]{1,0:T(8,128)(2,1)S(1)}, u32[]{:S(2)}, u32[]{:S(2)}) collective-permute-start(bf16[256,128]{1,0:T(8,128)(2,1)S(1)} %get-tuple-element.44), channel_id=1, source_target_pairs={{7,0},{0,1},{1,2},{2,3},{3,4},{4,5},{5,6},{6,7},{15,8},{8,9},{9,10... | collective-permute-start | bytes 196616 | tf_op jit(solution)/shard_map/ppermute | solution.py:98
  74.0 5.5 %collective-permute-start.29 = (bf16[304,128]{1,0:T(8,128)(2,1)S(1)}, bf16[304,128]{1,0:T(8,128)(2,1)S(1)}, u32[]{:S(2)}, u32[]{:S(2)}) collective-permute-start(bf16[304,128]{1,0:T(8,128)(2,1)S(1)} %shard_map.159.refs_0_), channel_id=1, source_target_pairs={{0,8},{2,10},{4,12},{6,14},{1,9},{3,11},{5,13},{7,15},{16,24},{18,... | collective-permute-start | bytes 233480 | tf_op jit(solution)/shard_map/ppermute | solution.py:572
  74.1 5.4 %collective-permute-start.32 = (bf16[304,128]{1,0:T(8,128)(2,1)S(1)}, bf16[304,128]{1,0:T(8,128)(2,1)S(1)}, u32[]{:S(2)}, u32[]{:S(2)}) collective-permute-start(bf16[304,128]{1,0:T(8,128)(2,1)S(1)} %collective-permute-done.28.refs_3_), channel_id=1, source_target_pairs={{0,8},{2,10},{4,12},{6,14},{1,9},{3,11},{5,13},{7,15},{16,24},{18,... | collective-permute-start | bytes 233480 | tf_op jit(solution)/shard_map/ppermute | solution.py:572
  74.5 5.0 %collective-permute-start.31 = (bf16[304,128]{1,0:T(8,128)(2,1)S(1)}, bf16[304,128]{1,0:T(8,128)(2,1)S(1)}, u32[]{:S(2)}, u32[]{:S(2)}) collective-permute-start(bf16[304,128]{1,0:T(8,128)(2,1)S(1)} %collective-permute-done.27.refs_2_), channel_id=1, source_target_pairs={{0,8},{2,10},{4,12},{6,14},{1,9},{3,11},{5,13},{7,15},{16,24},{18,... | collective-permute-start | bytes 233480 | tf_op jit(solution)/shard_map/ppermute | solution.py:572
  74.6 4.8 %collective-permute-start.30 = (bf16[304,128]{1,0:T(8,128)(2,1)S(1)}, bf16[304,128]{1,0:T(8,128)(2,1)S(1)}, u32[]{:S(2)}, u32[]{:S(2)}) collective-permute-start(bf16[304,128]{1,0:T(8,128)(2,1)S(1)} %collective-permute-done.26.refs_1_), channel_id=1, source_target_pairs={{0,8},{2,10},{4,12},{6,14},{1,9},{3,11},{5,13},{7,15},{16,24},{18,... | collective-permute-start | bytes 233480 | tf_op jit(solution)/shard_map/ppermute | solution.py:572
